TPU v7x, 32 devices: a whole 2x2x4 slice. The times are simulated.
32 devices in a mesh: dom: 8 (over z, x), sub: 4 (over y, core).
Axes of the slice: x: 2, y: 2, z: 4, core: 2. Of those that a mesh axis runs over, the one named last changes fastest.
Arguments:
- positions: float32 [3, 262144], P(None, ('dom', 'sub')), may hold values from 0 to 1
- masses: float32 [262144], P(('dom', 'sub')), may hold values from 0.00029296876 to 0.0029296875
- cell_mass: float32 [4096], P(('dom', 'sub')), may hold values from 0.00234375 to 0.0234375
- cell_center: float32 [3, 4096], P(None, ('dom', 'sub')), may hold values from 0 to 1
- cell_quad: float32 [6, 4096], P(None, ('dom', 'sub')), may hold values from -0.0046875 to 0.0046875
- cell_list: int32 [4096, 128], P(('dom', 'sub')), may hold values from 0 to 4095
- leaf_list: int32 [4096, 16], P(('dom', 'sub')), may hold values from 0 to 575, as said below
- send_list: int32 [8, 4, 8, 8], P('dom', 'sub'), may hold values from 0 to 127
- send_count: int32 [8, 4, 8], P('dom', 'sub'), may hold values from 1 to 8, as said below
Outputs:
- accel: float32 [3, 262144], P(None, ('dom', 'sub'))
Inputs may be any that keep to these rules, and one draw needn't show every extreme that they name: `send_count`: counts fall off with the distance along the curve: an offset of one domain always carries 8 blocks, an offset of d domains at most max(1, 8 // d). `leaf_list`: each id names a block of the group's own domain or a slot of the far part that carries a block.
All inputs are finite; a program needn't handle non-finite values.
Results may differ from a plain program's by a relative error of at most 0.0003.
Values sent between devices are 32-bit elements; how exact they have to be, the bound alone decides.
No kernel may reach another device: no remote copies, remote signals or barrier semaphores. Data moves between devices by JAX's collectives and lax.ppermute only.
A program may use at most 128 MiB of HBM per device.

v0:
```python
import jax
import jax.numpy as jnp
from jax import lax
from jax.sharding import PartitionSpec as P

LEAF = 64
LEAF_DEV = 128
NCELL = 128
NLEAF = 16
RANGE = 4
CAP = 8


softening_sq = 0.0025


def passed_along(value, axis, steps):
    count = lax.axis_size(axis)
    leading, last = (max(0, -steps), min(count, count - steps))
    return lax.ppermute(value, axis, [(source, source + steps) for source in range(leading, last)])


def direct_pull(targets, sources, weights):
    offset = sources[:, :, None, :] - targets[:, :, :, None]
    dist_sq = jnp.sum(offset * offset, axis=0) + softening_sq
    factor = weights[:, None, :] / (dist_sq * jnp.sqrt(dist_sq))
    return jnp.sum(offset * factor[None], axis=-1)


def multipole_pull(targets, moments):
    offset = targets[:, :, :, None] - moments[1:4, :, None, :]
    dist_sq = jnp.sum(offset * offset, axis=0) + softening_sq
    inv_one = 1.0 / jnp.sqrt(dist_sq)
    inv_two = inv_one * inv_one
    inv_three = inv_one * inv_two
    inv_five = inv_three * inv_two
    inv_seven = inv_five * inv_two
    quad_part = moments[4:10, :, None, :]
    q_times_x = quad_part[0] * offset[0] + quad_part[3] * offset[1] + quad_part[4] * offset[2]
    q_times_y = quad_part[3] * offset[0] + quad_part[1] * offset[1] + quad_part[5] * offset[2]
    q_times_z = quad_part[4] * offset[0] + quad_part[5] * offset[1] + quad_part[2] * offset[2]
    q_times = jnp.stack([q_times_x, q_times_y, q_times_z])
    quad_form = jnp.sum(offset * q_times, axis=0)
    mass_part = moments[0, :, None, :]
    accel_terms = (
        -mass_part * inv_three * offset + inv_five * q_times - 2.5 * inv_seven * quad_form * offset
    )
    return jnp.sum(accel_terms, axis=-1)


def group_pull(targets, essential, leaf_ids, cell_table, cell_ids):
    groups_here = leaf_ids.shape[0]
    particle_ids = (
        leaf_ids[:, :, None] * LEAF + jnp.arange(LEAF, dtype=jnp.int32)[None, None, :]
    ).reshape(groups_here, -1)
    picked = essential[:, particle_ids]
    moments = cell_table[:, cell_ids]
    return direct_pull(targets, picked[0:3], picked[3]) + multipole_pull(targets, moments)


def on_device(
    positions,
    masses,
    cell_mass,
    cell_center,
    cell_quad,
    cell_list,
    leaf_list,
    send_list,
    send_count,
):
    offset_values = list(range(-RANGE, 0)) + list(range(1, RANGE + 1))
    cell_table = jnp.concatenate([cell_mass[None], cell_center, cell_quad], axis=0)
    all_cells = lax.all_gather(cell_table, ("dom", "sub"), axis=1, tiled=True)
    packed = jnp.concatenate([positions, masses[None]], axis=0)
    nearby = lax.all_gather(packed, "sub", axis=1, tiled=True)
    chosen = send_list.reshape(2 * RANGE, CAP)
    counts = send_count.reshape(2 * RANGE)
    live = (jnp.arange(CAP, dtype=jnp.int32)[None, :] < counts[:, None]).astype(jnp.float32)
    weight = jnp.repeat(live.reshape(-1), LEAF).reshape(2 * RANGE, CAP * LEAF)
    flat_ids = (
        chosen[:, :, None] * LEAF + jnp.arange(LEAF, dtype=jnp.int32)[None, None, :]
    ).reshape(2 * RANGE, CAP * LEAF)
    outgoing = packed[:, flat_ids] * weight[None]
    pieces = []
    for slot in range(2 * RANGE):
        pieces.append(passed_along(outgoing[:, slot], "dom", offset_values[slot]))
    remote = jnp.stack(pieces, axis=1)
    essential = jnp.concatenate([nearby, remote.reshape(4, 2 * RANGE * CAP * LEAF)], axis=1)
    block_size = 8
    block_count = LEAF_DEV // block_size
    target_blocks = positions.reshape(3, block_count, block_size, LEAF).transpose(1, 0, 2, 3)
    leaf_blocks = leaf_list.reshape(block_count, block_size, NLEAF)
    cell_blocks = cell_list.reshape(block_count, block_size, NCELL)

    def one_block(inputs):
        block_targets, block_leaves, block_cells = inputs
        return group_pull(block_targets, essential, block_leaves, all_cells, block_cells)

    pulled = lax.map(one_block, (target_blocks, leaf_blocks, cell_blocks))
    return pulled.transpose(1, 0, 2, 3).reshape(3, LEAF_DEV * LEAF)


def solution(mesh):
    return jax.shard_map(
        on_device,
        mesh=mesh,
        in_specs=(
            P(None, ("dom", "sub")),
            P(("dom", "sub")),
            P(("dom", "sub")),
            P(None, ("dom", "sub")),
            P(None, ("dom", "sub")),
            P(("dom", "sub"), None),
            P(("dom", "sub"), None),
            P("dom", "sub", None, None),
            P("dom", "sub", None),
        ),
        out_specs=P(None, ("dom", "sub")),
        check_vma=False,
    )
```

profile of v0, /device:TPU:0, one launch (start us, length us, event | category | flops | bytes accessed | tf_op | source)
XLA Modules:
  0.0 815.5 jit_solution(4372808201360709425)
XLA Ops:
  4.0 12.9 %gather_fusion.2 = f32[4096,4]{1,0:T(8,128)S(1)} fusion(f32[4,8192]{0,1:T(8,128)} %copy.47, s32[4096]{0:T(1024)S(1)} %broadcast_clamp_fusion), kind=kCustom, calls=%fused_computation.2 | custom fusion | bytes 147456 | tf_op jit(solution)/shard_map/gather | solution.py:84
  23.0 5.5 collective-permute-start.4
  28.5 7.7 all_gather.6
  36.3 4.6 collective-permute-start.5
  40.9 6.3 collective-permute-start.6
  49.2 37.8 %all_gather.7 = f32[10,4096]{1,0:T(8,128)S(1)} all-gather(f32[10,128]{1,0:T(8,128)S(1)} %pad_maximum_fusion.3), channel_id=1, replica_groups=mesh['dom'=8,'sub'=4] {'dom','sub'}, dimensions={1}, use_global_device_ids=true | all-gather | bytes 168960 | tf_op jit(solution)/shard_map/all_gather | solution.py:74
  88.4 9.9 %copy.56 = f32[4,36864]{0,1:T(8,128)} copy(f32[4,36864]{1,0:T(4,128)S(1)} %pad_maximum_fusion.1) | data formatting | bytes 1179648 | tf_op jit(solution)/shard_map/while | solution.py:100
  98.3 716.4 %while.10 = (s32[]{:T(128)}, f32[16,3,8,64]{3,2,1,0:T(8,128)S(1)}, s32[16,8,16]{2,1,0:T(8,128)S(1)}, f32[4,36864]{0,1:T(8,128)}, f32[16,3,8,64]{3,2,0,1:T(8,128)...) while((s32[]{:T(128)}, f32[16,3,8,64]{3,2,1,0:T(8,128)S(1)}, ...), condition=%wide.region_6.7_spmd, body=%wide.region_0.6_spmd.sunk | while | flops 15249026 | bytes 16653933 | solution.py:100
  98.6 34.1 %gather_fusion = f32[8192,4]{1,0:T(8,128)} fusion(f32[4,36864]{0,1:T(8,128)} %get-tuple-element.193, s32[8192]{0:T(1024)S(1)} %bitcast_clamp_fusion.2), kind=kCustom, calls=%fused_computation.clone.1 | custom fusion | bytes 294912 | tf_op jit(solution)/shard_map/while/body/eval_jaxpr/gather | solution.py:56
  132.7 2.9 copy.69
  143.3 34.1 %gather_fusion = f32[8192,4]{1,0:T(8,128)} fusion(f32[4,36864]{0,1:T(8,128)} %get-tuple-element.193, s32[8192]{0:T(1024)S(1)} %bitcast_clamp_fusion.2), kind=kCustom, calls=%fused_computation.clone.1 | custom fusion | bytes 294912 | tf_op jit(solution)/shard_map/while/body/eval_jaxpr/gather | solution.py:56
  177.5 2.9 copy.69
  188.1 34.1 %gather_fusion = f32[8192,4]{1,0:T(8,128)} fusion(f32[4,36864]{0,1:T(8,128)} %get-tuple-element.193, s32[8192]{0:T(1024)S(1)} %bitcast_clamp_fusion.2), kind=kCustom, calls=%fused_computation.clone.1 | custom fusion | bytes 294912 | tf_op jit(solution)/shard_map/while/body/eval_jaxpr/gather | solution.py:56
  222.2 2.9 copy.69
  232.9 34.1 %gather_fusion = f32[8192,4]{1,0:T(8,128)} fusion(f32[4,36864]{0,1:T(8,128)} %get-tuple-element.193, s32[8192]{0:T(1024)S(1)} %bitcast_clamp_fusion.2), kind=kCustom, calls=%fused_computation.clone.1 | custom fusion | bytes 294912 | tf_op jit(solution)/shard_map/while/body/eval_jaxpr/gather | solution.py:56
  267.0 2.9 copy.69
  277.7 34.1 %gather_fusion = f32[8192,4]{1,0:T(8,128)} fusion(f32[4,36864]{0,1:T(8,128)} %get-tuple-element.193, s32[8192]{0:T(1024)S(1)} %bitcast_clamp_fusion.2), kind=kCustom, calls=%fused_computation.clone.1 | custom fusion | bytes 294912 | tf_op jit(solution)/shard_map/while/body/eval_jaxpr/gather | solution.py:56
  311.8 2.9 copy.69
  322.5 34.1 %gather_fusion = f32[8192,4]{1,0:T(8,128)} fusion(f32[4,36864]{0,1:T(8,128)} %get-tuple-element.193, s32[8192]{0:T(1024)S(1)} %bitcast_clamp_fusion.2), kind=kCustom, calls=%fused_computation.clone.1 | custom fusion | bytes 294912 | tf_op jit(solution)/shard_map/while/body/eval_jaxpr/gather | solution.py:56
  356.6 2.9 copy.69
  367.2 34.1 %gather_fusion = f32[8192,4]{1,0:T(8,128)} fusion(f32[4,36864]{0,1:T(8,128)} %get-tuple-element.193, s32[8192]{0:T(1024)S(1)} %bitcast_clamp_fusion.2), kind=kCustom, calls=%fused_computation.clone.1 | custom fusion | bytes 294912 | tf_op jit(solution)/shard_map/while/body/eval_jaxpr/gather | solution.py:56
  401.3 2.9 copy.69
  412.0 34.1 %gather_fusion = f32[8192,4]{1,0:T(8,128)} fusion(f32[4,36864]{0,1:T(8,128)} %get-tuple-element.193, s32[8192]{0:T(1024)S(1)} %bitcast_clamp_fusion.2), kind=kCustom, calls=%fused_computation.clone.1 | custom fusion | bytes 294912 | tf_op jit(solution)/shard_map/while/body/eval_jaxpr/gather | solution.py:56
  456.8 34.1 %gather_fusion = f32[8192,4]{1,0:T(8,128)} fusion(f32[4,36864]{0,1:T(8,128)} %get-tuple-element.193, s32[8192]{0:T(1024)S(1)} %bitcast_clamp_fusion.2), kind=kCustom, calls=%fused_computation.clone.1 | custom fusion | bytes 294912 | tf_op jit(solution)/shard_map/while/body/eval_jaxpr/gather | solution.py:56
  501.6 34.1 %gather_fusion = f32[8192,4]{1,0:T(8,128)} fusion(f32[4,36864]{0,1:T(8,128)} %get-tuple-element.193, s32[8192]{0:T(1024)S(1)} %bitcast_clamp_fusion.2), kind=kCustom, calls=%fused_computation.clone.1 | custom fusion | bytes 294912 | tf_op jit(solution)/shard_map/while/body/eval_jaxpr/gather | solution.py:56
  546.3 34.1 %gather_fusion = f32[8192,4]{1,0:T(8,128)} fusion(f32[4,36864]{0,1:T(8,128)} %get-tuple-element.193, s32[8192]{0:T(1024)S(1)} %bitcast_clamp_fusion.2), kind=kCustom, calls=%fused_computation.clone.1 | custom fusion | bytes 294912 | tf_op jit(solution)/shard_map/while/body/eval_jaxpr/gather | solution.py:56
  591.1 34.1 %gather_fusion = f32[8192,4]{1,0:T(8,128)} fusion(f32[4,36864]{0,1:T(8,128)} %get-tuple-element.193, s32[8192]{0:T(1024)S(1)} %bitcast_clamp_fusion.2), kind=kCustom, calls=%fused_computation.clone.1 | custom fusion | bytes 294912 | tf_op jit(solution)/shard_map/while/body/eval_jaxpr/gather | solution.py:56
  635.9 34.1 %gather_fusion = f32[8192,4]{1,0:T(8,128)} fusion(f32[4,36864]{0,1:T(8,128)} %get-tuple-element.193, s32[8192]{0:T(1024)S(1)} %bitcast_clamp_fusion.2), kind=kCustom, calls=%fused_computation.clone.1 | custom fusion | bytes 294912 | tf_op jit(solution)/shard_map/while/body/eval_jaxpr/gather | solution.py:56
  680.7 34.1 %gather_fusion = f32[8192,4]{1,0:T(8,128)} fusion(f32[4,36864]{0,1:T(8,128)} %get-tuple-element.193, s32[8192]{0:T(1024)S(1)} %bitcast_clamp_fusion.2), kind=kCustom, calls=%fused_computation.clone.1 | custom fusion | bytes 294912 | tf_op jit(solution)/shard_map/while/body/eval_jaxpr/gather | solution.py:56
  714.8 2.9 copy.69
  725.5 34.1 %gather_fusion = f32[8192,4]{1,0:T(8,128)} fusion(f32[4,36864]{0,1:T(8,128)} %get-tuple-element.193, s32[8192]{0:T(1024)S(1)} %bitcast_clamp_fusion.2), kind=kCustom, calls=%fused_computation.clone.1 | custom fusion | bytes 294912 | tf_op jit(solution)/shard_map/while/body/eval_jaxpr/gather | solution.py:56
  770.2 34.1 %gather_fusion = f32[8192,4]{1,0:T(8,128)} fusion(f32[4,36864]{0,1:T(8,128)} %get-tuple-element.193, s32[8192]{0:T(1024)S(1)} %bitcast_clamp_fusion.2), kind=kCustom, calls=%fused_computation.clone.1 | custom fusion | bytes 294912 | tf_op jit(solution)/shard_map/while/body/eval_jaxpr/gather | solution.py:56
  (455 shorter events, 159.5 us)
Async XLA Ops:
  0.0 3.7 copy-start.3
  0.0 17.6 %copy-start.6 = (s32[1,1,8]{2,1,0:T(1,128)S(1)}, s32[1,1,8]{2,1,0:T(1,128)}, u32[]{:S(2)}) copy-start(s32[1,1,8]{2,1,0:T(1,128)} %param.19) | copy-start | bytes 100
  1.0 35.2 %copy-start.4 = (f32[6,128]{1,0:T(8,128)S(1)}, f32[6,128]{1,0:T(8,128)}, u32[]{:S(2)}) copy-start(f32[6,128]{1,0:T(8,128)} %param.15) | copy-start | bytes 9220
  1.0 35.2 %copy-start.5 = (f32[3,128]{1,0:T(4,128)S(1)}, f32[3,128]{1,0:T(4,128)}, u32[]{:S(2)}) copy-start(f32[3,128]{1,0:T(4,128)} %param.14) | copy-start | bytes 4612
  1.0 35.2 %copy-start.7 = (f32[128]{0:T(128)S(1)}, f32[128]{0:T(128)}, u32[]{:S(2)}) copy-start(f32[128]{0:T(128)} %param.13) | copy-start | bytes 1540
  1.1 85.9 %copy-start = (f32[3,8192]{1,0:T(4,128)S(1)}, f32[3,8192]{1,0:T(4,128)}, u32[]{:S(2)}) copy-start(f32[3,8192]{1,0:T(4,128)} %param.11) | copy-start | bytes 294916
  1.1 86.1 %copy-start.2 = (s32[128,16]{0,1:T(8,128)S(1)}, s32[128,16]{0,1:T(8,128)}, u32[]{:S(2)}) copy-start(s32[128,16]{0,1:T(8,128)} %param.17) | copy-start | bytes 24580
  17.8 18.4 %collective-permute-start = (f32[4,512]{1,0:T(4,128)S(1)}, f32[4,512]{1,0:T(4,128)S(1)}, u32[]{:S(2)}, u32[]{:S(2)}) collective-permute-start(f32[4,512]{1,0:T(4,128)S(1)} %get-tuple-element.100), channel_id=1, source_target_pairs={{16,0},{20,4},{24,8},{28,12},{17,1},{21,5},{25,9},{29,13},{18,2},{... | collective-permute-start | bytes 24584 | tf_op jit(solution)/shard_map/ppermute | solution.py:20
  19.1 21.8 %collective-permute-start.1 = (f32[4,512]{1,0:T(4,128)S(1)}, f32[4,512]{1,0:T(4,128)S(1)}, u32[]{:S(2)}, u32[]{:S(2)}) collective-permute-start(f32[4,512]{1,0:T(4,128)S(1)} %get-tuple-element.99), channel_id=1, source_target_pairs={{12,0},{16,4},{20,8},{24,12},{28,16},{13,1},{17,5},{21,9},{25,13},... | collective-permute-start | bytes 24584 | tf_op jit(solution)/shard_map/ppermute | solution.py:20
  20.4 26.8 %collective-permute-start.2 = (f32[4,512]{1,0:T(4,128)S(1)}, f32[4,512]{1,0:T(4,128)S(1)}, u32[]{:S(2)}, u32[]{:S(2)}) collective-permute-start(f32[4,512]{1,0:T(4,128)S(1)} %get-tuple-element.98), channel_id=1, source_target_pairs={{8,0},{12,4},{16,8},{20,12},{24,16},{28,20},{9,1},{13,5},{17,9},{2... | collective-permute-start | bytes 24584 | tf_op jit(solution)/shard_map/ppermute | solution.py:20
  21.7 66.2 %collective-permute-start.3 = (f32[4,512]{1,0:T(4,128)S(1)}, f32[4,512]{1,0:T(4,128)S(1)}, u32[]{:S(2)}, u32[]{:S(2)}) collective-permute-start(f32[4,512]{1,0:T(4,128)S(1)} %get-tuple-element.97), channel_id=1, source_target_pairs={{4,0},{8,4},{12,8},{16,12},{20,16},{24,20},{28,24},{5,1},{9,5},{13... | collective-permute-start | bytes 24584 | tf_op jit(solution)/shard_map/ppermute | solution.py:20
  23.0 64.9 %collective-permute-start.4 = (f32[4,512]{1,0:T(4,128)S(1)}, f32[4,512]{1,0:T(4,128)S(1)}, u32[]{:S(2)}, u32[]{:S(2)}) collective-permute-start(f32[4,512]{1,0:T(4,128)S(1)} %get-tuple-element.96), channel_id=1, source_target_pairs={{0,4},{4,8},{8,12},{12,16},{16,20},{20,24},{24,28},{1,5},{5,9},{9,... | collective-permute-start | bytes 24584 | tf_op jit(solution)/shard_map/ppermute | solution.py:20
  36.3 51.7 %collective-permute-start.5 = (f32[4,512]{1,0:T(4,128)S(1)}, f32[4,512]{1,0:T(4,128)S(1)}, u32[]{:S(2)}, u32[]{:S(2)}) collective-permute-start(f32[4,512]{1,0:T(4,128)S(1)} %get-tuple-element.95), channel_id=1, source_target_pairs={{0,8},{4,12},{8,16},{12,20},{16,24},{20,28},{1,9},{5,13},{9,17},{1... | collective-permute-start | bytes 24584 | tf_op jit(solution)/shard_map/ppermute | solution.py:20
  40.9 47.1 %collective-permute-start.6 = (f32[4,512]{1,0:T(4,128)S(1)}, f32[4,512]{1,0:T(4,128)S(1)}, u32[]{:S(2)}, u32[]{:S(2)}) collective-permute-start(f32[4,512]{1,0:T(4,128)S(1)} %get-tuple-element.94), channel_id=1, source_target_pairs={{0,12},{4,16},{8,20},{12,24},{16,28},{1,13},{5,17},{9,21},{13,25},... | collective-permute-start | bytes 24584 | tf_op jit(solution)/shard_map/ppermute | solution.py:20
  47.2 40.9 %collective-permute-start.7 = (f32[4,512]{1,0:T(4,128)S(1)}, f32[4,512]{1,0:T(4,128)S(1)}, u32[]{:S(2)}, u32[]{:S(2)}) collective-permute-start(f32[4,512]{1,0:T(4,128)S(1)} %get-tuple-element.93), channel_id=1, source_target_pairs={{0,16},{4,20},{8,24},{12,28},{1,17},{5,21},{9,25},{13,29},{2,18},{... | collective-permute-start | bytes 24584 | tf_op jit(solution)/shard_map/ppermute | solution.py:20
  88.4 9.9 %copy-start.1 = (f32[16,3,8,64]{3,2,1,0:T(8,128)S(1)}, f32[16,3,8,64]{3,2,1,0:T(8,128)}, u32[]{:S(2)}) copy-start(f32[16,3,8,64]{3,2,1,0:T(8,128)} %custom-call.6) | copy-start | bytes 294916
where the time goes:
time: 817 us; the launch traced here: 815 us
  local copies, waits for them, and re-layouts  672 us (82%)
  other arithmetic  71.9 us (9%)
  blocking collectives  45.6 us (6%)
  starting transfers between devices  23.5 us (3%)
    gather x32, local copies, waits for them, and re-layouts, group_pull(): picked = essential[:, particle_ids]  591 us
    gather x32, local copies, waits for them, and re-layouts, group_pull(): moments = cell_table[:, cell_ids]  47.8 us
    all_gather x1, blocking collectives, on_device(): all_cells = lax.all_gather(cell_table, ('dom', 'sub'), axis=1, tiled=True)  37.8 us
    ppermute x8, starting transfers between devices, passed_along(): lax.ppermute(value, axis, [(source, source + steps) for source in range(l...  23.5 us
  transfers between devices with their start and end apart: 8, of which 0 were waited for; matrix products, arithmetic and copies ran while one was open for 0% of the time, Pallas kernels for 0%

commit v1 on v0

v1 whole, which is shorter than its diff:
```python
import functools

import jax
import jax.numpy as jnp
from jax import lax
from jax.experimental import pallas as pl
from jax.experimental.pallas import tpu as pltpu
from jax.sharding import PartitionSpec as P

LEAF = 64
LEAF_DEV = 128
NCELL = 128
NLEAF = 16
RANGE = 4
CAP = 8
PAIRS = LEAF_DEV // 2
CELL_UNITS = 3
OUT_UNITS = CAP // 2
OFFSETS = list(range(-RANGE, 0)) + list(range(1, RANGE + 1))

softening_sq = 0.0025
GRID_ROUND = 49152.0
F32 = jnp.float32
BF16 = jnp.bfloat16

H_ROWS = 32
Q_ROWS = 64
V_ROWS = 16
U_ROWS = 48
Q_AT = H_ROWS
V_AT = Q_AT + Q_ROWS
U_AT = V_AT + V_ROWS
CELL_ROWS = U_AT + U_ROWS
SOURCE_ROWS = H_ROWS + V_ROWS


def rounded(value):
    return value.astype(BF16).astype(F32)


def three_parts(value):
    first = rounded(value)
    rest = value - first
    second = rounded(rest)
    return first, second, rest - second


def two_parts(value):
    first = value.astype(BF16)
    return first, (value - first.astype(F32)).astype(BF16)


def grid_parts(value):
    high = (value + GRID_ROUND) - GRID_ROUND
    low = value - high
    first = rounded(low)
    return high, low, first, low - first


def norm_parts(parts, extra=None):
    big = sum(high * high for high, _, _, _ in parts)
    small = sum(low * (2.0 * high + low) for high, low, _, _ in parts)
    if extra is not None:
        small = small + extra
    return three_parts(big), three_parts(small)


def pack_kernel(pos_ref, mass_ref, cmass_ref, center_ref, quad_ref, out_ref):
    for pair in range(PAIRS):
        lanes = pl.ds(128 * pair, 128)
        out_ref[pair, 0:3, :] = pos_ref[:, lanes]
        out_ref[pair, 3:4, :] = mass_ref[:, lanes]
    out_ref[PAIRS, 0:1, :] = cmass_ref[...]
    out_ref[PAIRS, 1:4, :] = center_ref[...]
    out_ref[PAIRS + 1] = quad_ref[0:4, :]
    out_ref[PAIRS + 2, 0:2, :] = quad_ref[4:6, :]
    out_ref[PAIRS + 2, 2:4, :] = jnp.zeros((2, 128), F32)


def outgoing_kernel(n_dom, n_sub, own_ref, all_ref, list_ref, count_ref, out_ref):
    me = lax.axis_index("dom")
    left = lax.broadcasted_iota(jnp.int32, (4, 128), 1) < LEAF
    zero = jnp.zeros((OUT_UNITS, 4, 128), F32)

    def one_target(target, carry):
        out_ref[target, 0:OUT_UNITS] = zero
        for seg in range(n_sub):
            at = OUT_UNITS + CELL_UNITS * seg
            out_ref[target, at : at + CELL_UNITS] = all_ref[seg, PAIRS : PAIRS + CELL_UNITS]
        return carry

    lax.fori_loop(0, n_dom, one_target, 0)

    def half(slot, j, right):
        block = list_ref[slot, j]
        value = own_ref[block // 2]
        value = jnp.where(j < count_ref[0, slot], value, 0.0)
        return jnp.where((block & 1) == right, value, pltpu.roll(value, LEAF, 1))

    for slot in range(2 * RANGE):
        target = me + OFFSETS[slot]

        @pl.when((target >= 0) & (target < n_dom))
        def _():
            for unit in range(OUT_UNITS):
                out_ref[target, unit] = jnp.where(left, half(slot, 2 * unit, 0), half(slot, 2 * unit + 1, 1))


def build_table(n_dom, n_sub, all_ref, recv_ref, tab_ref):
    left = lax.broadcasted_iota(jnp.int32, (4, 128), 1) < LEAF

    def put(at, value):
        turned = pltpu.roll(value, LEAF, 1)
        tab_ref[at] = jnp.where(left, value, turned)
        tab_ref[at + 1] = jnp.where(left, turned, value)

    for seg in range(n_sub):

        def near(step, carry):
            for sub in range(8):
                pair = step * 8 + sub
                put(seg * LEAF_DEV + 2 * pair, all_ref[seg, pair])
            return carry

        lax.fori_loop(0, PAIRS // 8, near, 0)
    me = lax.axis_index("dom")
    for slot in range(2 * RANGE):
        source = me - OFFSETS[slot]
        inside = (source >= 0) & (source < n_dom)
        source = jnp.clip(source, 0, n_dom - 1)
        for unit in range(OUT_UNITS):
            value = jnp.where(inside, recv_ref[source, unit], 0.0)
            put(n_sub * LEAF_DEV + slot * CAP + 2 * unit, value)


def target_features(all_ref, tg_ref, ce_ref, feat_ref, ah_ref, aq_ref):
    me = lax.axis_index("sub")
    left = lax.broadcasted_iota(jnp.int32, (8, 128), 1) < LEAF
    one = jnp.ones((8, 128), F32)
    zero = jnp.zeros((8, 128), F32)
    raw_ref = tg_ref

    def copy_in(pair, carry):
        raw_ref[pl.ds(pl.multiple_of(4 * pair, 4), 4), :] = all_ref[me, pair]
        return carry

    lax.fori_loop(0, PAIRS, copy_in, 0)

    def one_octet(octet, carry):
        parts, centred = [], []
        for comp in range(3):
            rows = pl.ds(octet * 32 + comp, 8, stride=4)
            value = raw_ref[rows, :]
            first = jnp.broadcast_to(value[:, 0:1], (8, 128))
            second = jnp.broadcast_to(value[:, LEAF : LEAF + 1], (8, 128))
            ce_ref[comp, pl.ds(octet * 16, 8, stride=2), :] = first
            ce_ref[comp, pl.ds(octet * 16 + 1, 8, stride=2), :] = second
            value = value - jnp.where(left, first, second)
            raw_ref[rows, :] = value
            centred.append(value)
            parts.append(grid_parts(value))
        big, small = norm_parts(parts, softening_sq)
        minus_high = [-2.0 * part[0] for part in parts]
        minus_one = [-2.0 * part[2] for part in parts]
        minus_two = [-2.0 * part[3] for part in parts]
        rows = minus_high + [one] * 3 + list(big) + minus_high + minus_one + minus_high
        rows += minus_two + minus_one + [one] * 3 + list(small) + [zero] * 2
        x, y, z = centred
        split = [three_parts(v) for v in (x, y, z, x * x, y * y, z * z, x * y, x * z, y * z)]
        for which in (0, 0, 1, 0, 1, 2):
            rows += [part[which] for part in split]
        rows += [one] * 3 + [zero] * 7
        for at, value in enumerate(rows):
            feat_ref[8 * at : 8 * at + 8, :] = value
        for sub in range(8):
            pair = octet * 8 + sub
            ah_ref[pair] = feat_ref[pl.ds(sub, H_ROWS, stride=8), :].T.astype(BF16)
            aq_ref[pair] = feat_ref[pl.ds(8 * H_ROWS + sub, Q_ROWS, stride=8), :].T.astype(BF16)
        return carry

    lax.fori_loop(0, PAIRS // 8, one_octet, 0)


def source_h_rows(parts):
    (p1, p2, p3), (s1, s2, s3) = norm_parts(parts)
    high = [part[0] for part in parts]
    one = [part[2] for part in parts]
    two = [part[3] for part in parts]
    rows = dict(enumerate(high + [p1, p2, p3]))
    rows.update(enumerate(one + high + two + high + one + [s1, s2, s3], 9))
    return rows


def put_rows(ref, rows):
    for at, value in rows.items():
        ref[8 * at : 8 * at + 8, :] = value


def fill_constant_rows(ref, count):
    one = jnp.ones((8, 128), F32)
    zero = jnp.zeros((8, 128), F32)
    for at in range(count):
        ones = at in (6, 7, 8, 27, 28, 29) or (count == CELL_ROWS and at == V_AT + 3)
        ref[8 * at : 8 * at + 8, :] = one if ones else zero


def cell_features(n_dom, n_sub, octet, cl_ref, recv_ref, ce_ref, cf_ref, cm_ref):
    ids = cl_ref[pl.ds(pl.multiple_of(8 * octet, 8), 8), :]
    lane = ids & 127
    owner = ids >> 7

    def one_domain(dom, found):
        for seg in range(n_sub):
            here = owner == dom * n_sub + seg
            at = OUT_UNITS + CELL_UNITS * seg
            new = []
            for comp in range(10):
                row = recv_ref[dom, at + comp // 4, comp % 4 : comp % 4 + 1, :]
                value = jnp.take_along_axis(jnp.broadcast_to(row, (8, 128)), lane, axis=1, mode="promise_in_bounds")
                new.append(jnp.where(here, value, found[comp]))
            found = tuple(new)
        return found

    start = tuple(jnp.zeros((8, 128), F32) for _ in range(10))
    mass, cx, cy, cz, xx, yy, zz, xy, xz, yz = lax.fori_loop(0, n_dom, one_domain, start)
    cm_ref[...] = mass
    rows8 = pl.ds(pl.multiple_of(8 * octet, 8), 8)
    cx, cy, cz = [value - ce_ref[comp, rows8, :] for comp, value in enumerate((cx, cy, cz))]
    put_rows(cf_ref, source_h_rows([grid_parts(value) for value in (cx, cy, cz)]))
    qx = xx * cx + xy * cy + xz * cz
    qy = xy * cx + yy * cy + yz * cz
    qz = xz * cx + yz * cy + zz * cz
    const = three_parts(2.5 * (qx * cx + qy * cy + qz * cz))
    linear = [-5.0 * qx, -5.0 * qy, -5.0 * qz]
    square = [2.5 * xx, 2.5 * yy, 2.5 * zz, 5.0 * xy, 5.0 * xz, 5.0 * yz]
    split = [three_parts(value) for value in linear + square]
    rows = []
    for which in (0, 1, 0, 2, 1, 0):
        rows += [part[which] for part in split]
    rows += list(const)
    put_rows(cf_ref, dict(enumerate(rows, Q_AT)))
    for comp, value in enumerate((cx, cy, cz)):
        for which, part in enumerate(three_parts(value)):
            cf_ref[8 * (V_AT + 4 * which + comp) : 8 * (V_AT + 4 * which + comp) + 8, :] = part
    columns = {name: three_parts(value) for name, value in dict(xx=xx, yy=yy, zz=zz, xy=xy, xz=xz, yz=yz, cx=qx, cy=qy, cz=qz).items()}
    order = (("xx", "xy", "xz"), ("xy", "yy", "yz"), ("xz", "yz", "zz"), ("cx", "cy", "cz"))
    for which in range(3):
        for column, names in enumerate(order):
            for row, name in enumerate(names):
                at = U_AT + 16 * which + 4 * column + row
                cf_ref[8 * at : 8 * at + 8, :] = columns[name][which]


def source_features(group, ll_ref, tab_ref, ce_ref, raw_ref, sf_ref):
    left = lax.broadcasted_iota(jnp.int32, (4, 128), 1) < LEAF
    for pair in range(NLEAF // 2):
        first = tab_ref[ll_ref[group, 2 * pair]]
        second = tab_ref[ll_ref[group, 2 * pair + 1]]
        raw_ref[4 * pair : 4 * pair + 4, :] = jnp.where(left, first, second)
    value = [raw_ref[pl.ds(comp, 8, stride=4), :] for comp in range(4)]
    mass = value[3]
    centred = [value[comp] - ce_ref[comp, pl.ds(group, 1), :] for comp in range(3)]
    put_rows(sf_ref, source_h_rows([grid_parts(v) for v in centred]))
    for comp, v in enumerate([mass * v for v in centred] + [mass]):
        for which, part in enumerate(three_parts(v)):
            at = H_ROWS + 4 * which + comp
            sf_ref[8 * at : 8 * at + 8, :] = part


def transposed_dot(rows, weights):
    return lax.dot_general(rows, weights, (((1,), (1,)), ((), ())), preferred_element_type=F32)


def summed(rows, value):
    high, low = two_parts(value)
    return transposed_dot(rows, high) + transposed_dot(rows, low)


def one_group(sub, target_h, target_q, sf_ref, cf_ref, cm_ref):
    total = jnp.zeros((V_ROWS, LEAF), F32)
    for block in range(4):
        pieces = [sf_ref[pl.ds(2 * block + half, H_ROWS, stride=8), :].astype(BF16) for half in range(2)]
        dist_sq = jnp.dot(target_h, jnp.concatenate(pieces, axis=1), preferred_element_type=F32)
        inv = lax.rsqrt(dist_sq)
        weights = [sf_ref[pl.ds(8 * H_ROWS + 2 * block + half, V_ROWS, stride=8), :].astype(BF16) for half in range(2)]
        total += summed(jnp.concatenate(weights, axis=1), inv * inv * inv)

    def cell_rows(at, count):
        return cf_ref[pl.ds(8 * at + sub, count, stride=8), :].astype(BF16)

    dist_sq = jnp.dot(target_h, cell_rows(0, H_ROWS), preferred_element_type=F32)
    quad_form = jnp.dot(target_q, cell_rows(Q_AT, Q_ROWS), preferred_element_type=F32)
    inv = lax.rsqrt(dist_sq)
    inv_two = inv * inv
    inv_three = inv * inv_two
    pull = inv_three * (cm_ref[pl.ds(sub, 1), :] + quad_form * (inv_two * inv_two))
    total += summed(cell_rows(V_AT, V_ROWS), pull)
    quad = summed(cell_rows(U_AT, U_ROWS), inv_three * inv_two)
    return total[0:8] + total[8:16], quad[0:16] + quad[16:32] + quad[32:48]


def pull_kernel(n_dom, n_sub, all_ref, recv_ref, cl_ref, ll_ref, out_ref, tab_ref, tg_ref, ce_ref, feat_ref, ah_ref, aq_ref, cf_ref, cm_ref, raw_ref, sf_ref):
    build_table(n_dom, n_sub, all_ref, recv_ref, tab_ref)
    target_features(all_ref, tg_ref, ce_ref, feat_ref, ah_ref, aq_ref)
    fill_constant_rows(cf_ref, CELL_ROWS)
    for half in range(2):
        fill_constant_rows(sf_ref.at[half], SOURCE_ROWS)
    upper = lax.broadcasted_iota(jnp.int32, (8, 128), 0) < 4

    def one_octet(octet, carry):
        cell_features(n_dom, n_sub, octet, cl_ref, recv_ref, ce_ref, cf_ref, cm_ref)

        def one_pair(inner, carry):
            pair = octet * 4 + inner
            sums, quads = [], []
            for half in range(2):
                source_features(2 * pair + half, ll_ref, tab_ref, ce_ref, raw_ref.at[half], sf_ref.at[half])
            for half in range(2):
                rows = pl.ds(LEAF * half, LEAF)
                sums_half, quads_half = one_group(
                    2 * inner + half, ah_ref[pair, rows, :], aq_ref[pair, rows, :], sf_ref.at[half], cf_ref, cm_ref
                )
                sums.append(sums_half)
                quads.append(quads_half)
            sums = jnp.concatenate(sums, axis=1)
            quads = jnp.concatenate(quads, axis=1)
            sums = sums + pltpu.roll(sums, 4, 0)
            place = tg_ref[pl.ds(pl.multiple_of(4 * pair, 4), 4), :]
            x, y, z = [place[comp : comp + 1, :] for comp in range(3)]
            turned = quads[0:8] * jnp.where(upper, x, y) + quads[8:16] * jnp.where(upper, z, -1.0)
            turned = turned + pltpu.roll(turned, 4, 0)
            result = sums + turned
            lanes = pl.ds(pl.multiple_of(128 * pair, 128), 128)
            out_ref[:, lanes] = result[0:3] - place[0:3] * sums[3:4]
            return carry

        lax.fori_loop(0, 4, one_pair, 0)
        return carry

    lax.fori_loop(0, LEAF_DEV // 8, one_octet, 0)


def on_device(n_dom, n_sub, positions, masses, cell_mass, cell_center, cell_quad, cell_list, leaf_list, send_list, send_count):
    vmem = pl.BlockSpec(memory_space=pltpu.VMEM)
    smem = pl.BlockSpec(memory_space=pltpu.SMEM)
    params = pltpu.CompilerParams(vmem_limit_bytes=48 * 1024 * 1024)
    packed = pl.pallas_call(
        pack_kernel,
        out_shape=jax.ShapeDtypeStruct((PAIRS + CELL_UNITS, 4, 128), F32),
        in_specs=[vmem] * 5,
        out_specs=vmem,
        compiler_params=params,
        name="pack_own",
    )(positions, masses.reshape(1, -1), cell_mass.reshape(1, -1), cell_center, cell_quad)
    nearby = lax.all_gather(packed, "sub", axis=0, tiled=False)
    units = OUT_UNITS + CELL_UNITS * n_sub
    outgoing = pl.pallas_call(
        functools.partial(outgoing_kernel, n_dom, n_sub),
        out_shape=jax.ShapeDtypeStruct((n_dom, units, 4, 128), F32),
        in_specs=[vmem, vmem, smem, smem],
        out_specs=vmem,
        compiler_params=params,
        name="pack_outgoing",
    )(packed, nearby, send_list.reshape(2 * RANGE, CAP), send_count.reshape(1, 2 * RANGE))
    received = lax.all_to_all(outgoing, "dom", split_axis=0, concat_axis=0, tiled=True)
    return pl.pallas_call(
        functools.partial(pull_kernel, n_dom, n_sub),
        out_shape=jax.ShapeDtypeStruct((3, LEAF_DEV * LEAF), F32),
        in_specs=[vmem, vmem, vmem, smem],
        out_specs=vmem,
        scratch_shapes=[
            pltpu.VMEM((n_sub * LEAF_DEV + 2 * RANGE * CAP, 4, 128), F32),
            pltpu.VMEM((4 * PAIRS, 128), F32),
            pltpu.VMEM((3, LEAF_DEV, 128), F32),
            pltpu.VMEM((8 * (H_ROWS + Q_ROWS), 128), F32),
            pltpu.VMEM((PAIRS, 128, H_ROWS), BF16),
            pltpu.VMEM((PAIRS, 128, Q_ROWS), BF16),
            pltpu.VMEM((8 * CELL_ROWS, 128), F32),
            pltpu.VMEM((8, 128), F32),
            pltpu.VMEM((2, 32, 128), F32),
            pltpu.VMEM((2, 8 * SOURCE_ROWS, 128), F32),
        ],
        compiler_params=params,
        name="pull",
    )(nearby, received, cell_list, leaf_list)


def solution(mesh):
    sharded = P(("dom", "sub"))
    return jax.shard_map(
        functools.partial(on_device, mesh.shape["dom"], mesh.shape["sub"]),
        mesh=mesh,
        in_specs=(
            P(None, ("dom", "sub")),
            sharded,
            sharded,
            P(None, ("dom", "sub")),
            P(None, ("dom", "sub")),
            P(("dom", "sub"), None),
            P(("dom", "sub"), None),
            P("dom", "sub", None, None),
            P("dom", "sub", None),
        ),
        out_specs=P(None, ("dom", "sub")),
        check_vma=False,
    )
```

time: 817 us -> 112 us (0.14)
  local copies, waits for them, and re-layouts: 672 us -> 3.83 us
  Pallas kernels: 0 us -> 83.5 us
  other arithmetic: 71.9 us -> 0 us
  blocking collectives: 45.6 us -> 8.78 us
  starting transfers between devices: 23.5 us -> 5.92 us
  waiting for transfers between devices: 0.02 us -> 9.31 us
    gather x66 -> x0, local copies, waits for them, and re-layouts: 653 us -> none  [the longest x32 591 us: group_pull(): picked = essential[:, particle_ids]]
    pallas_call x0 -> x3, Pallas kernels: none -> 83.5 us  [the longest x1 81.6 us: on_device(): pl.pallas_call(functools.partial(pull_kernel, n_dom, n_sub), out_shape=ja...]
    reduce_sum x64 -> x0, other arithmetic: 38.1 us -> none  [the longest x16 14 us: direct_pull(): return jnp.sum(offset * factor[None], axis=-1)]
    all_gather x2 -> x1, blocking collectives: 45.6 us -> 8.78 us  [on_device(): nearby = lax.all_gather(packed, 'sub', axis=0, tiled=False)]
    ppermute x8 -> x0, starting transfers between devices: 23.5 us -> none  [passed_along(): lax.ppermute(value, axis, [(source, source + steps) for source in range(l...]
    div x16 -> x0, other arithmetic: 12.2 us -> none  [direct_pull(): factor = weights[:, None, :] / (dist_sq * jnp.sqrt(dist_sq))]
    gather x33 -> x0, other arithmetic: 11.4 us -> none  [the longest x16 11.2 us: group_pull(): moments = cell_table[:, cell_ids]]
    while x2 -> x0, local copies, waits for them, and re-layouts: 10.5 us -> none  [on_device(): pulled = lax.map(one_block, (target_blocks, leaf_blocks, cell_blocks))]
  transfers between devices with their start and end apart: 8 -> 1, of which waited for: 0 -> 1; matrix products, arithmetic and copies ran while one was open for 0% -> 0% of each run, Pallas kernels for 0% -> 0%
where the time goes in v1:
time: 112 us; the launch traced here: 111 us
  Pallas kernels  83.5 us (75%)
  waiting for transfers between devices  9.31 us (8%)
  blocking collectives  8.78 us (8%)
  starting transfers between devices  5.92 us (5%)
  local copies, waits for them, and re-layouts  3.83 us (3%)
    pallas_call x1, Pallas kernels, on_device(): pl.pallas_call(functools.partial(pull_kernel, n_dom, n_sub), out_shape=ja...  81.6 us
    all_to_all x1, waiting for transfers between devices, on_device(): lax.all_to_all(outgoing, 'dom', split_axis=0, concat_axis=0, tiled=True)  9.31 us
    all_gather x1, blocking collectives, on_device(): nearby = lax.all_gather(packed, 'sub', axis=0, tiled=False)  8.78 us
    all_to_all x1, starting transfers between devices, on_device(): lax.all_to_all(outgoing, 'dom', split_axis=0, concat_axis=0, tiled=True)  5.92 us
    unnamed x19, local copies, waits for them, and re-layouts  3.83 us
  transfers between devices with their start and end apart: 1, of which 1 were waited for; matrix products, arithmetic and copies ran while one was open for 0% of the time, Pallas kernels for 0%

profile of v1, /device:TPU:0, one launch (start us, length us, event | category | flops | bytes accessed | tf_op | source)
XLA Modules:
  0.0 111.4 jit_solution(13893878277512377922)
XLA Ops:
  0.0 0.0 copy-start.5
  0.0 0.0 copy-start.7
  0.0 0.7 copy-done.5
  0.7 0.0 copy-done.7
  0.7 0.0 copy-start
  0.7 0.9 copy-done
  1.6 0.0 copy-start.2
  1.6 0.8 copy-done.2
  2.3 0.0 copy-start.3
  2.4 0.7 copy-done.3
  3.1 8.8 %all-gather = f32[268,4,128]{2,1,0:T(4,128)S(1)} all-gather(f32[67,4,128]{2,1,0:T(4,128)S(1)} %pack_own.1.own_ref), channel_id=2, replica_groups=mesh['dom'=8,'sub'=4] {'sub'}, dimensions={0}, use_global_device_ids=true | all-gather | bytes 686080 | tf_op jit(solution)/shard_map/all_gather | solution.py:355
  11.9 0.0 copy-start.4
  11.9 0.0 copy-start.6
  11.9 0.7 copy-done.4
  12.6 0.0 copy-done.6
  12.6 1.8 %pack_outgoing.1 = f32[8,16,4,128]{3,2,1,0:T(4,128)} custom-call(f32[67,4,128]{2,1,0:T(4,128)S(1)} %pack_own.1.own_ref, f32[4,67,4,128]{3,2,1,0:T(4,128)S(1)} %bitcast.5, s32[8,8]{1,0:T(8,128)S(1)} %bitcast.8, s32[1,8]{1,0:T(1,128)S(1)} %bitcast.9), custom_call_target="tpu_custom_call" | custom-call | tf_op jit(solution)/shard_map/pack_outgoing/pallas_call | solution.py:357
  14.4 0.0 copy-start.8
  14.4 5.9 %all-to-all-start = ((f32[8,16,4,128]{3,2,1,0:T(4,128)}), f32[8,16,4,128]{3,2,1,0:T(4,128)S(1)}, u32[]{:S(2)}, u32[]{:S(2)}) async-start(f32[8,16,4,128]{3,2,1,0:T(4,128)} %pack_outgoing.1), calls=%async_computation | async-start | bytes 524288 | tf_op jit(solution)/shard_map/all_to_all | solution.py:365
  20.3 0.0 copy-done.8
  20.3 0.0 copy-start.1
  20.3 0.1 copy.11.ll_ref
  20.4 9.3 %all-to-all-done.recv_ref = f32[8,16,4,128]{3,2,1,0:T(4,128)S(1)} async-done(((f32[8,16,4,128]{3,2,1,0:T(4,128)}), f32[8,16,4,128]{3,2,1,0:T(4,128)S(1)}, u32[]{:S(2)}, u32[]{:S(2)}) %all-to-all-start) | async-done | bytes 262176 | tf_op jit(solution)/shard_map/all_to_all | solution.py:365
  29.7 0.0 copy-done.1
  29.7 81.6 %pull.1 = f32[3,8192]{1,0:T(4,128)} custom-call(f32[4,67,4,128]{3,2,1,0:T(4,128)S(1)} %bitcast.6, f32[8,16,4,128]{3,2,1,0:T(4,128)S(1)} %all-to-all-done.recv_ref, s32[128,128]{1,0:T(8,128)S(1)} %copy-done.1, s32[128,16]{1,0:T(8,128)S(1)} %copy.11.ll_ref), custom_call_target="tpu_custom_call" | custom-call | tf_op jit(solution)/shard_map/pull/pallas_call | solution.py:366
  (1 shorter events, 0.0 us)
Async XLA Ops:
  0.0 0.7 copy-start.5
  0.0 0.7 copy-start.7
  0.7 0.9 copy-start
  1.6 0.8 copy-start.2
  2.3 0.7 copy-start.3
  11.9 0.7 copy-start.4
  11.9 0.7 copy-start.6
  14.4 5.9 %copy-start.8 = (s32[128,16]{0,1:T(8,128)S(1)}, s32[128,16]{0,1:T(8,128)}, u32[]{:S(2)}) copy-start(s32[128,16]{0,1:T(8,128)} %param.15) | copy-start | bytes 24580
  14.4 15.4 %all-to-all-start = ((f32[8,16,4,128]{3,2,1,0:T(4,128)}), f32[8,16,4,128]{3,2,1,0:T(4,128)S(1)}, u32[]{:S(2)}, u32[]{:S(2)}) async-start(f32[8,16,4,128]{3,2,1,0:T(4,128)} %pack_outgoing.1), calls=%async_computation | async-start | bytes 524288 | tf_op jit(solution)/shard_map/all_to_all | solution.py:365
  20.3 9.4 %copy-start.1 = (s32[128,128]{1,0:T(8,128)S(1)}, s32[128,128]{1,0:T(8,128)}, u32[]{:S(2)}) copy-start(s32[128,128]{1,0:T(8,128)} %cl_ref.1) | copy-start | bytes 196612
